TPU v7x, 512 devices: a whole 4x8x8 slice. The times are simulated.
512 devices in a mesh: layer: 64 (over z, y), tok: 8 (over x, core).
Axes of the slice: x: 4, y: 8, z: 8, core: 2. Of those that a mesh axis runs over, the one named last changes fastest.
Arguments:
- states: bfloat16 [64, 1024, 1024], P('layer', 'tok'), may hold values from -6 to 6
- w_qkv: bfloat16 [128, 1024, 1536], P('layer', 'tok'), may hold values from -12 to 12
- w_out: bfloat16 [128, 512, 1024], P('layer', 'tok'), may hold values from -0.25 to 0.25
- gains: float32 [128, 1024], P('layer'), may hold values from 0.5 to 1.5
- coarse_gain: float32 [64, 1024], P('layer'), may hold values from 0.85 to 1
- doc_ids: int32 [1024], P('tok'), may hold values from 0 to 3, never falling along the last dimension, each value on 1 to 512 neighbouring positions
Outputs:
- corrected: float32 [64, 1024, 1024], P('layer', 'tok')
- ends: float32 [64, 1024, 1024], P('layer', 'tok')
Inputs may be any that keep to these rules, and one draw needn't show every extreme that they name: `doc_ids`: document numbers never fall along the tokens; each document has 1 to 512 tokens and one has exactly 512.
All inputs are finite; a program needn't handle non-finite values.
Results may differ from a plain program's by a relative error of at most 0.0065.
Values may be sent and summed in bfloat16 or wider, within the bound.
A program may use at most 128 MiB of HBM per device.

v0:
```python
import jax
import jax.numpy as jnp
from jax import lax
from jax.sharding import PartitionSpec as P

HEAD_DIM = 64


def from_behind(value, axis, steps):
    count = lax.axis_size(axis)
    initial, last = (max(0, -steps), min(count, count - steps))
    return lax.ppermute(value, axis, [(source, source + steps) for source in range(initial, last)])


def entering(value, axis, join, neutral):
    count, mine = (lax.axis_size(axis), lax.axis_index(axis))
    pieces = jax.tree.map(lambda part: lax.all_gather(part, axis), value)
    total = jax.tree.map(
        lambda part, zero: jnp.full_like(part, 0) + jnp.asarray(zero, part.dtype), value, neutral
    )

    def lap(position, total):
        longer = join(total, jax.tree.map(lambda part: part[position], pieces))
        return jax.tree.map(lambda new, old: jnp.where(position < mine, new, old), longer, total)

    return lax.fori_loop(0, count - 1, lap, total)


def combine(earlier, later):
    return (later[0] * earlier[0], later[0] * earlier[1] + later[1])


def attention(query, keys, values, allowed, head_dim):
    scores = jnp.einsum("qhd,khd->hqk", query, keys, preferred_element_type=jnp.float32) / jnp.sqrt(
        jnp.float32(head_dim)
    )
    scores = jnp.where(allowed[None], scores, -1e30)
    peak = jnp.max(scores, axis=2, keepdims=True)
    expo = jnp.where(allowed[None], jnp.exp(scores - peak), 0.0)
    probs = (expo / jnp.sum(expo, axis=2, keepdims=True)).astype(jnp.bfloat16)
    return jnp.einsum("hqk,khd->qhd", probs, values, preferred_element_type=jnp.float32)


def per_device(states, w_qkv, w_out, gains, coarse_gain, doc_ids):
    tok_dev = states.shape[1]
    depth = w_qkv.shape[0]
    width = w_qkv.shape[2] // 3
    head_dim = HEAD_DIM
    heads = width // head_dim
    all_ids = lax.all_gather(doc_ids, "tok", axis=0, tiled=True)
    total = all_ids.shape[0]
    every_pos = jnp.arange(total, dtype=jnp.int32)
    follow = from_behind(states, "layer", -1)[0]
    query_pos = lax.axis_index("tok") * tok_dev + jnp.arange(tok_dev, dtype=jnp.int32)
    allowed = (every_pos[None, :] <= query_pos[:, None]) & (all_ids[None, :] == doc_ids[:, None])
    state = states[0].astype(jnp.float32)
    for inner in range(depth):
        mean_square = jnp.mean(state * state, axis=1, keepdims=True)
        normed = (state * lax.rsqrt(mean_square + 1e-05) * gains[inner][None, :]).astype(
            jnp.bfloat16
        )
        qkv = jnp.dot(
            normed,
            lax.all_gather(w_qkv[inner], "tok", axis=0, tiled=True),
            preferred_element_type=jnp.float32,
        ).astype(jnp.bfloat16)
        query = qkv[:, :width].reshape(tok_dev, heads, head_dim)
        keys, values = (
            lax.all_gather(qkv[:, width : 2 * width], "tok", axis=0, tiled=True),
            lax.all_gather(qkv[:, 2 * width :], "tok", axis=0, tiled=True),
        )
        keys = keys.reshape(total, heads, head_dim)
        values = values.reshape(total, heads, head_dim)
        mixed = attention(query, keys, values, allowed, head_dim)
        mixed = mixed.reshape(tok_dev, width).astype(jnp.bfloat16)
        update = jnp.dot(
            mixed,
            lax.all_gather(w_out[inner], "tok", axis=0, tiled=True),
            preferred_element_type=jnp.float32,
        )
        state = state + update
    residual = state - follow.astype(jnp.float32)
    identity = (jnp.ones_like(coarse_gain), jnp.zeros_like(residual))
    prefix_gain, error = entering((coarse_gain, residual), "layer", combine, identity)
    corrected = states[0].astype(jnp.float32) + error
    ends = state + coarse_gain * error
    return (corrected[None], ends[None])


def solution(mesh):
    in_specs = (
        P("layer", "tok", None),
        P("layer", "tok", None),
        P("layer", "tok", None),
        P("layer", None),
        P("layer", None),
        P("tok"),
    )
    out_specs = (P("layer", "tok", None), P("layer", "tok", None))
    return jax.shard_map(
        per_device, mesh=mesh, in_specs=in_specs, out_specs=out_specs, check_vma=False
    )
```

profile of v0, /device:TPU:1, one launch (start us, length us, event | category | flops | bytes accessed | tf_op | source)
XLA Modules:
  0.0 602.4 jit_solution(12015302983439393506)
XLA Ops:
  7.2 2.1 fusion.46
  11.3 38.5 %all-gather.26.cloned.1.call-done = bf16[1,1024,1536]{2,1,0:T(8,128)(2,1)} async-done(((bf16[1,128,1536]{2,1,0:T(8,128)(2,1)}), bf16[1,1024,1536]{2,1,0:T(8,128)(2,1)}) %all-gather.26.cloned.1.call-update) | async-done | bytes 3145744 | tf_op jit(solution)/shard_map/all_gather | solution.py:64
  49.7 2.6 fusion.9
  55.3 9.4 %all-gather.7 = s32[8,1,128]{2,1,0:T(1,128)S(1)} all-gather(s32[1,1,128]{2,1,0:T(1,128)S(1)} %bitcast.91), channel_id=1, replica_groups=mesh['layer'=64,'tok'=8] {'tok'}, dimensions={0}, use_global_device_ids=true | all-gather | bytes 4608 | tf_op jit(solution)/shard_map/all_gather | solution.py:50
  65.0 17.2 %all-gather.20.cloned.1.call-done = bf16[1024,512]{1,0:T(8,128)(2,1)} async-done(((bf16[128,512]{1,0:T(8,128)(2,1)}), bf16[1024,512]{1,0:T(8,128)(2,1)}) %all-gather.20.cloned.1.call-update) | async-done | bytes 1048592 | tf_op jit(solution)/shard_map/all_gather | solution.py:69
  82.2 1.5 copy.22
  83.7 29.3 %all-gather.18.cloned.1.call-done = bf16[1024,512]{1,0:T(8,128)(2,1)} async-done(((bf16[128,512]{1,0:T(8,128)(2,1)}), bf16[1024,512]{1,0:T(8,128)(2,1)}) %all-gather.18.cloned.1.call-update) | async-done | bytes 1048592 | tf_op jit(solution)/shard_map/all_gather | solution.py:70
  113.0 1.5 copy.20
  114.5 3.9 fusion.51
  118.4 3.1 fusion.24
  121.5 22.1 %all-gather.28.cloned.1.call-done = bf16[1,512,1024]{2,1,0:T(8,128)(2,1)} async-done(((bf16[1,64,1024]{2,1,0:T(8,128)(2,1)}), bf16[1,512,1024]{2,1,0:T(8,128)(2,1)}) %all-gather.28.cloned.1.call-update) | async-done | bytes 1048592 | tf_op jit(solution)/shard_map/all_gather | solution.py:78
  143.7 1.6 multiply_reduce_fusion
  145.3 33.7 %all-gather.30.cloned.1.call-done = bf16[1,1024,1536]{2,1,0:T(8,128)(2,1)} async-done(((bf16[1,128,1536]{2,1,0:T(8,128)(2,1)}), bf16[1,1024,1536]{2,1,0:T(8,128)(2,1)}) %all-gather.30.cloned.1.call-update) | async-done | bytes 3145744 | tf_op jit(solution)/shard_map/all_gather | solution.py:64
  179.1 2.5 fusion.12
  185.3 26.1 %all-gather.24.cloned.1.call-done = bf16[1024,512]{1,0:T(8,128)(2,1)} async-done(((bf16[128,512]{1,0:T(8,128)(2,1)}), bf16[1024,512]{1,0:T(8,128)(2,1)}) %all-gather.24.cloned.1.call-update) | async-done | bytes 1048592 | tf_op jit(solution)/shard_map/all_gather | solution.py:69
  211.5 1.5 copy.25
  213.0 29.9 %all-gather.22.cloned.1.call-done = bf16[1024,512]{1,0:T(8,128)(2,1)} async-done(((bf16[128,512]{1,0:T(8,128)(2,1)}), bf16[1024,512]{1,0:T(8,128)(2,1)}) %all-gather.22.cloned.1.call-update) | async-done | bytes 1048592 | tf_op jit(solution)/shard_map/all_gather | solution.py:70
  242.8 1.5 copy.23
  244.3 3.9 fusion.52
  248.2 3.1 fusion.23
  251.3 22.3 %all-gather.32.cloned.1.call-done = bf16[1,512,1024]{2,1,0:T(8,128)(2,1)} async-done(((bf16[1,64,1024]{2,1,0:T(8,128)(2,1)}), bf16[1,512,1024]{2,1,0:T(8,128)(2,1)}) %all-gather.32.cloned.1.call-update) | async-done | bytes 1048592 | tf_op jit(solution)/shard_map/all_gather | solution.py:78
  273.6 2.4 convert_subtract_fusion
  276.0 41.5 %all-gather.6 = f32[64,1,1024]{2,1,0:T(1,128)S(1)} all-gather(f32[1,1,1024]{2,1,0:T(1,128)S(1)} %bitcast.86), channel_id=2, replica_groups=mesh['layer'=64,'tok'=8] {'layer'}, dimensions={0}, use_global_device_ids=true | all-gather | bytes 266240 | tf_op jit(solution)/shard_map/all_gather | solution.py:17
  317.6 181.5 %all-gather.34.cloned.1.call-done = f32[8192,1024]{1,0:T(8,128)} async-done(((f32[128,1024]{1,0:T(8,128)}), f32[8192,1024]{1,0:T(8,128)}) %all-gather.34.cloned.1.call-update) | async-done | bytes 33554448 | tf_op jit(solution)/shard_map/all_gather | solution.py:17
  499.1 95.7 %while.14 = (s32[]{:T(128)}, f32[128,1024]{1,0:T(8,128)S(1)}, s32[]{:T(128)}, f32[64,1,1024]{2,1,0:T(1,128)S(1)}, f32[64,128,1024]{2,1,0:T(8,128)}, /*index=5*/s32[]{:T(128)}, s32[]{:T(128)}) while((s32[]{:T(128)}, f32[128,1024]{1,0:T(8,128)S(1)}, s32[]{:T(128)}, f32[64,1,1024]{2,1,0:T(1,128)S(1)}, f32[64,128,1024]{2,1,0:T(8,128)}, ...), condition=%wide.region_7.8_spmd.clone, body=%wide.region_6.7_spmd.clone.sunk | while | flops 524292 | bytes 1585257 | solution.py:26
  500.6 1.5 fusion.66
  502.1 1.5 fusion.66
  503.7 1.5 fusion.66
  505.2 1.5 fusion.66
  506.7 1.5 fusion.66
  508.2 1.5 fusion.66
  509.7 1.5 fusion.66
  511.2 1.5 fusion.66
  512.8 1.5 fusion.66
  514.3 1.5 fusion.66
  515.8 1.5 fusion.66
  517.3 1.5 fusion.66
  518.8 1.5 fusion.66
  520.4 1.5 fusion.66
  521.9 1.5 fusion.66
  523.4 1.5 fusion.66
  524.9 1.5 fusion.66
  526.4 1.5 fusion.66
  528.0 1.5 fusion.66
  529.5 1.5 fusion.66
  531.0 1.5 fusion.66
  532.5 1.5 fusion.66
  534.0 1.5 fusion.66
  535.6 1.5 fusion.66
  537.1 1.5 fusion.66
  538.6 1.5 fusion.66
  540.1 1.5 fusion.66
  541.6 1.5 fusion.66
  543.2 1.5 fusion.66
  544.7 1.5 fusion.66
  549.2 1.5 fusion.66
  553.8 1.5 fusion.66
  558.4 1.5 fusion.66
  562.9 1.5 fusion.66
  573.5 1.5 fusion.66
  578.1 1.5 fusion.66
  582.7 1.5 fusion.66
  587.2 1.5 fusion.66
  591.8 1.5 fusion.66
  (128 shorter events, 46.0 us)
Async XLA Ops:
  7.2 46.7 %copy-start.1 = (bf16[2,64,1024]{2,1,0:T(8,128)(2,1)S(1)}, bf16[2,64,1024]{2,1,0:T(8,128)(2,1)}, u32[]{:S(2)}) copy-start(bf16[2,64,1024]{2,1,0:T(8,128)(2,1)} %param.10) | copy-start | bytes 786436
  7.2 48.1 %copy-start.3 = (s32[128]{0:T(128)S(1)}, s32[128]{0:T(128)}, u32[]{:S(2)}) copy-start(s32[128]{0:T(128)} %param.13) | copy-start | bytes 1540
  7.2 42.5 %all-gather.26.cloned.1.call-start = ((), (), s32[]{:S(2)}) async-start(), calls=%async_computation.4 | async-start | bytes 3538944 | tf_op jit(solution)/shard_map/all_gather | solution.py:64
  9.3 72.9 %all-gather.20.cloned.1.call-start = ((), (), s32[]{:S(2)}) async-start(), calls=%async_computation.1 | async-start | bytes 1179648 | tf_op jit(solution)/shard_map/all_gather | solution.py:69
  53.1 59.9 %all-gather.18.cloned.1.call-start = ((), (), s32[]{:S(2)}) async-start(), calls=%async_computation | async-start | bytes 1179648 | tf_op jit(solution)/shard_map/all_gather | solution.py:70
  53.9 89.8 %all-gather.28.cloned.1.call-start = ((), (), s32[]{:S(2)}) async-start(), calls=%async_computation.5 | async-start | bytes 1179648 | tf_op jit(solution)/shard_map/all_gather | solution.py:78
  54.7 124.4 %all-gather.30.cloned.1.call-start = ((), (), s32[]{:S(2)}) async-start(), calls=%async_computation.6 | async-start | bytes 3538944 | tf_op jit(solution)/shard_map/all_gather | solution.py:64
  55.3 156.2 %all-gather.24.cloned.1.call-start = ((), (), s32[]{:S(2)}) async-start(), calls=%async_computation.3 | async-start | bytes 1179648 | tf_op jit(solution)/shard_map/all_gather | solution.py:69
  118.4 25.3 %copy-start = (bf16[1,128,1024]{2,1,0:T(8,128)(2,1)S(1)}, bf16[1,128,1024]{2,1,0:T(8,128)(2,1)}, u32[]{:S(2)}) copy-start(bf16[1,128,1024]{2,1,0:T(8,128)(2,1)} %param.8) | copy-start | bytes 786436
  182.4 60.5 %all-gather.22.cloned.1.call-start = ((), (), s32[]{:S(2)}) async-start(), calls=%async_computation.2 | async-start | bytes 1179648 | tf_op jit(solution)/shard_map/all_gather | solution.py:70
  183.1 90.5 %all-gather.32.cloned.1.call-start = ((), (), s32[]{:S(2)}) async-start(), calls=%async_computation.7 | async-start | bytes 1179648 | tf_op jit(solution)/shard_map/all_gather | solution.py:78
  183.9 315.2 %all-gather.34.cloned.1.call-start = ((), (), s32[]{:S(2)}) async-start(), calls=%async_computation.8 | async-start | bytes 34078720 | tf_op jit(solution)/shard_map/all_gather | solution.py:17
  183.9 67.4 %collective-permute-start = (bf16[1,128,1024]{2,1,0:T(8,128)(2,1)S(1)}, bf16[1,128,1024]{2,1,0:T(8,128)(2,1)S(1)}, u32[]{:S(2)}, u32[]{:S(2)}) collective-permute-start(bf16[1,128,1024]{2,1,0:T(8,128)(2,1)S(1)} %copy-done), channel_id=1, source_target_pairs={{8,0},{16,8},{24,16},{32,24},{40,32},{48,40},{56,48},{64,56},{72,6... | collective-permute-start | bytes 786440 | tf_op jit(solution)/shard_map/ppermute | solution.py:12
  248.2 27.8 %copy-start.2 = (f32[1,1024]{1,0:T(1,128)S(1)}, f32[1,1024]{1,0:T(1,128)}, u32[]{:S(2)}) copy-start(f32[1,1024]{1,0:T(1,128)} %param.12) | copy-start | bytes 12292
Sparse Core Ops, SparseCore 0:
  10.7 38.9 all-gather.25
  53.2 28.9 all-gather.19
  84.4 28.5 all-gather.17
  115.0 28.5 all-gather.27
  146.2 32.8 all-gather.29
  182.5 28.9 all-gather.23
  214.2 28.5 all-gather.21
  245.0 28.5 all-gather.31
  277.3 221.7 all-gather.33
where the time goes:
time: 606 us; the launch traced here: 602 us
  waiting for transfers between devices  403 us (67%)
  other arithmetic  95.8 us (16%)
  blocking collectives  50.9 us (8%)
  matrix products  23.1 us (4%)
  between operations  14 us (2%)
  local copies, waits for them, and re-layouts  11.7 us (2%)
    all_gather x1, waiting for transfers between devices, entering(): pieces = jax.tree.map(lambda part: lax.all_gather(part, axis), value)  182 us
    select_n x63, other arithmetic, lap(): jnp.where(position < mine, new, old)  93.4 us
    all_gather x2, waiting for transfers between devices, per_device(): lax.all_gather(w_qkv[inner], 'tok', axis=0, tiled=True)  72.2 us
    all_gather x2, waiting for transfers between devices, per_device(): lax.all_gather(qkv[:, 2 * width:], 'tok', axis=0, tiled=True)  59.2 us
    all_gather x2, waiting for transfers between devices, per_device(): lax.all_gather(w_out[inner], 'tok', axis=0, tiled=True)  44.4 us
    all_gather x2, waiting for transfers between devices, per_device(): lax.all_gather(qkv[:, width:2 * width], 'tok', axis=0, tiled=True)  43.3 us
    all_gather x1, blocking collectives, entering(): pieces = jax.tree.map(lambda part: lax.all_gather(part, axis), value)  41.5 us
  transfers between devices with their start and end apart: 10, of which 9 were waited for; matrix products, arithmetic and copies ran while one was open for 4% of the time, Pallas kernels for 0%

commit v1 on v0

v1 whole, which is shorter than its diff:
```python
import math

import jax
import jax.numpy as jnp
from jax import lax
from jax.experimental import pallas as pl
from jax.experimental.pallas import tpu as pltpu
from jax.sharding import PartitionSpec as P

MESH = pl.DeviceIdType.MESH
D = 1024
NX = 4
NB = 8
RING = 8
CHUNKS = 2
EXP2_SCALE = math.log2(math.e) / 8.0
FAR_FIRST = (4, 3, 5, 2, 6, 1, 7)


def rms(value, gain):
    mean_square = jnp.mean(value * value, axis=1, keepdims=True)
    return (value * lax.rsqrt(mean_square + 1e-05) * gain).astype(jnp.bfloat16)


def make_kernel(ny, nz):
    cw = D // CHUNKS

    def kernel(
        states, w_qkv, w_out, gains, coarse, doc_ids,
        c_out, d_out,
        sx, wq, wo, kv, q2, o1, o2s, o2, x2, nx2, bias, docs,
        gy, pz, dsend, drecv, trecv, csend, crecv,
        loc, w_ss, w_rs, wr_ss, wr_rs, s_ss, s_rs, doc_ss, doc_rs,
        wo_ss, wo_rs, wor_ss, wor_rs, kv_ss, kv_rs, o1_ss, o1_rs, o2_ss, o2_rs,
        g_ss, g_rs, p_ss, p_rs, y1_ss, y1_rs, z_ss, z_rs, y2_ss, y2_rs,
    ):
        layer, tok = lax.axis_index("layer"), lax.axis_index("tok")
        x, c = tok // 2, tok % 2
        z, y = layer // ny, layer % ny
        sibling = (layer, 2 * x + 1 - c)

        def chip(delta):
            return (x + delta) % NX

        def at_x(delta):
            return (layer, 2 * chip(delta) + c)

        def at_y(delta):
            return (z * ny + (y + delta) % ny, tok)

        def at_z(delta):
            return (((z + delta) % nz) * ny + y, tok)

        ydeltas = [k for k in FAR_FIRST if k < ny]
        zdeltas = [k for k in FAR_FIRST if k < nz]
        sends = []

        def remote(src, dst, ss, rs, device):
            copy = pltpu.make_async_remote_copy(
                src_ref=src, dst_ref=dst, send_sem=ss, recv_sem=rs,
                device_id=device, device_id_type=MESH,
            )
            return copy

        def send(*args):
            copy = remote(*args)
            copy.start()
            sends.append(copy)
            return copy

        own_state = pltpu.make_async_copy(states.at[0], sx.at[x], loc.at[0])
        own_state.start()
        own_wq = [[], []]
        own_wo = []
        for inner in range(2):
            for part in range(3):
                copy = pltpu.make_async_copy(
                    w_qkv.at[inner, :, pl.ds(pl.multiple_of(part * 512 + 128 * x, 128), 128)],
                    wq.at[inner, x, c, :, pl.ds(128 * part, 128)],
                    loc.at[1 + 3 * inner + part],
                )
                copy.start()
                own_wq[inner].append(copy)
            copy = pltpu.make_async_copy(w_out.at[inner], wo.at[inner, x, c], loc.at[7 + inner])
            copy.start()
            own_wo.append(copy)
        docs[tok] = doc_ids[...]
        gy[y] = coarse[...]

        barrier = pltpu.get_barrier_semaphore()
        partners = [sibling] + [at_x(k) for k in (2, 1, 3)]
        partners += [at_y(k) for k in ydeltas] + [at_z(k) for k in zdeltas]
        for partner in partners:
            pl.semaphore_signal(barrier, inc=1, device_id=partner, device_id_type=MESH)
        pl.semaphore_wait(barrier, len(partners))

        def send_wq(inner):
            found = []
            for delta in (2, 1, 3):
                for part in range(3):
                    found.append(send(
                        w_qkv.at[inner, :, pl.ds(pl.multiple_of(part * 512 + 128 * chip(delta), 128), 128)],
                        wq.at[inner, x, c, :, pl.ds(128 * part, 128)],
                        w_ss.at[inner, delta, part], w_rs.at[inner, delta, part], at_x(delta),
                    ))
            return found

        def share_wq(inner, arriving):
            for copy in own_wq[inner]:
                copy.wait()
            for copy in arriving:
                copy.wait_recv()
            return send(wq.at[inner, :, c], wq.at[inner, :, c], wr_ss.at[inner], wr_rs.at[inner], sibling)

        def send_wo(inner):
            return [
                send(w_out.at[inner], wo.at[inner, x, c], wo_ss.at[inner, k], wo_rs.at[inner, k], at_x(k))
                for k in (2, 1, 3)
            ]

        def share_wo(inner, arriving):
            own_wo[inner].wait()
            for copy in arriving:
                copy.wait_recv()
            return send(wo.at[inner, :, c], wo.at[inner, :, c], wor_ss.at[inner], wor_rs.at[inner], sibling)

        wq_coming = send_wq(0)
        doc_coming = [
            send(doc_ids, docs.at[tok], doc_ss.at[k], doc_rs.at[k], at_x(k)) for k in (2, 1, 3)
        ]

        def half(delta, number):
            rows = pl.ds(64 * number, 64)
            return send(
                states.at[0, rows], sx.at[x, rows], s_ss.at[delta, number], s_rs.at[delta, number], at_x(delta)
            )

        from_left_0, from_right_1 = half(1, 0), half(3, 1)
        from_left_1, from_right_0 = half(1, 1), half(3, 0)
        gain_coming = [send(coarse, gy.at[y], g_ss.at[k], g_rs.at[k], at_y(k)) for k in ydeltas]

        for copy in doc_coming:
            copy.wait_recv()
        doc_shared = [
            send(docs.at[2 * k + c], docs.at[2 * k + c], doc_ss.at[4 + k], doc_rs.at[4 + k], sibling)
            for k in range(NX)
        ]
        for copy in gain_coming:
            copy.wait_recv()
        product = gy[0]
        for k in range(1, ny):
            product = product * gy[k]
        pz[z] = product
        product_coming = [send(pz.at[z], pz.at[z], p_ss.at[k], p_rs.at[k], at_z(k)) for k in zdeltas]
        for copy in doc_shared:
            copy.wait_recv()

        key_first = [0, 0, c, 2 + c]
        key_blocks = [2, 4, 5, 5]
        row = lax.broadcasted_iota(jnp.int32, (128, 128), 0)
        lane = lax.broadcasted_iota(jnp.int32, (128, 128), 1)
        for j in range(NX):
            block = 2 * j + c
            mine = docs[block].astype(jnp.float32)
            mine = jnp.broadcast_to(mine, (128, 128)).T
            for k in range(key_blocks[j]):
                other = key_first[j] + k
                theirs = docs[other].astype(jnp.float32)
                allowed = (mine == theirs) & (lane + 128 * (other - block) <= row)
                bias[j, :, 128 * k : 128 * (k + 1)] = jnp.where(allowed, 0.0, -1e30)

        wq_shared = share_wq(0, wq_coming)

        from_left_0.wait_recv()
        left_two = send(
            sx.at[chip(3), pl.ds(0, 64)], sx.at[chip(3), pl.ds(0, 64)], s_ss.at[2, 0], s_rs.at[2, 0], at_x(1)
        )
        from_right_1.wait_recv()
        right_two = send(
            sx.at[chip(1), pl.ds(64, 64)], sx.at[chip(1), pl.ds(64, 64)], s_ss.at[2, 1], s_rs.at[2, 1], at_x(3)
        )
        wo_coming = send_wo(0)
        wq_shared.wait_recv()
        own_state.wait()

        kv_shared = [[], []]

        def keep_qkv(inner, j, qkv):
            head = lax.broadcasted_iota(jnp.int32, (128, 128), 1) < 64
            query = qkv[:, :128]
            q2[j, :128] = jnp.where(head, query, 0.0).astype(jnp.bfloat16)
            q2[j, 128:] = jnp.where(head, 0.0, query).astype(jnp.bfloat16)
            block = 2 * j + c
            kv[inner, block] = qkv[:, 128:].astype(jnp.bfloat16)

        def first_qkv(delta):
            j = chip(delta)
            normed = rms(sx[j].astype(jnp.float32), gains[0:1, :])
            qkv = jnp.dot(normed, wq[0].reshape(D, 384), preferred_element_type=jnp.float32)
            keep_qkv(0, j, qkv)
            block = 2 * j + c
            kv_shared[0].append(
                send(kv.at[0, block], kv.at[0, block], kv_ss.at[0, delta], kv_rs.at[0, delta], sibling)
            )

        first_qkv(0)
        from_left_1.wait_recv()
        first_qkv(3)
        from_right_0.wait_recv()
        first_qkv(1)
        left_two.wait_recv()
        right_two.wait_recv()
        first_qkv(2)

        def attention(inner, j):
            count = 128 * key_blocks[j]
            keys = pl.ds(key_first[j], key_blocks[j])
            k = kv[inner, keys, :, :128].reshape(count, 128)
            v = kv[inner, keys, :, 128:].reshape(count, 128)
            scores = lax.dot_general(
                q2[j], k, (((1,), (1,)), ((), ())), preferred_element_type=jnp.float32
            )
            scores = (scores.reshape(2, 128, count) + bias[j, :, :count][None]).reshape(256, count)
            peak = jnp.max(scores, axis=1, keepdims=True)
            expo = jnp.exp2((scores - peak) * EXP2_SCALE)
            total = jnp.sum(expo, axis=1, keepdims=True)
            probs = (expo * (1.0 / total)).astype(jnp.bfloat16)
            mixed = jnp.dot(probs, v, preferred_element_type=jnp.float32)
            head = lax.broadcasted_iota(jnp.int32, (128, 128), 1) < 64
            return jnp.where(head, mixed[:128], mixed[128:]).astype(jnp.bfloat16)

        for copy in kv_shared[0]:
            copy.wait_recv()
        o1_coming = []
        for j in range(NX):
            o1[x, j] = attention(0, j)
            o1_coming.append([
                send(o1.at[x, j], o1.at[x, j], o1_ss.at[j, k], o1_rs.at[j, k], at_x(k)) for k in (2, 1, 3)
            ])
        wq_coming = send_wq(1)
        wo_shared = share_wo(0, wo_coming)
        wo_coming = send_wo(1)
        wo_shared.wait_recv()

        for j in range(NX):
            for copy in o1_coming[j]:
                copy.wait_recv()
            heads = jnp.concatenate([o1[k, j] for k in range(NX)], axis=1)
            value = sx[j].astype(jnp.float32) + jnp.dot(
                heads, wo[0].reshape(512, D), preferred_element_type=jnp.float32
            )
            x2[j] = value
            nx2[j] = rms(value, gains[1:2, :])

        share_wq(1, wq_coming).wait_recv()
        for j in range(NX):
            qkv = jnp.dot(nx2[j], wq[1].reshape(D, 384), preferred_element_type=jnp.float32)
            keep_qkv(1, j, qkv)
            block = 2 * j + c
            kv_shared[1].append(
                send(kv.at[1, block], kv.at[1, block], kv_ss.at[1, j], kv_rs.at[1, j], sibling)
            )
        for copy in kv_shared[1]:
            copy.wait_recv()
        home = []
        for j in range(NX):
            o2s[j] = attention(1, j)
            copy = remote(o2s.at[j], o2.at[x], o2_ss.at[j], o2_rs.at[x], (layer, 2 * j + c))
            home.append(copy)

            @pl.when(x != j)
            def _(copy=copy):
                copy.start()

        o2[x] = o2s[x]
        share_wo(1, wo_coming).wait_recv()
        for delta in (1, 2, 3):
            pltpu.make_async_copy(o2s.at[0], o2.at[chip(delta)], o2_rs.at[chip(delta)]).wait()
        heads = jnp.concatenate([o2[k] for k in range(NX)], axis=1)
        value = x2[x] + jnp.dot(heads, wo[1].reshape(512, D), preferred_element_type=jnp.float32)
        start = jnp.where(layer == 0, 0.0, sx[x].astype(jnp.float32))
        value = value - coarse[...] * start
        d_out[...] = value
        dsend[...] = value.astype(jnp.bfloat16)

        def columns(chunk):
            return pl.ds(cw * chunk, cw)

        def rows_of(position):
            return pl.ds(pl.multiple_of(16 * position, 16), 16)

        y1_coming = [
            [
                send(
                    dsend.at[rows_of((y + k) % ny), columns(chunk)], drecv.at[y, :, columns(chunk)],
                    y1_ss.at[chunk, k], y1_rs.at[chunk, k], at_y(k),
                )
                for k in ydeltas
            ]
            for chunk in range(CHUNKS)
        ]
        drecv[y] = dsend[rows_of(y), :]
        for copy in product_coming:
            copy.wait_recv()
        z_coming = []
        for chunk in range(CHUNKS):
            for copy in y1_coming[chunk]:
                copy.wait_recv()
            total = jnp.zeros((16, cw), jnp.float32)
            for k in range(ny):
                total = gy[k, :, columns(chunk)] * total + drecv[k, :, columns(chunk)].astype(jnp.float32)
            trecv[z, :, columns(chunk)] = total.astype(jnp.bfloat16)
            z_coming.append([
                send(
                    trecv.at[z, :, columns(chunk)], trecv.at[z, :, columns(chunk)],
                    z_ss.at[chunk, k], z_rs.at[chunk, k], at_z(k),
                )
                for k in zdeltas
            ])
        y2_coming = []
        for chunk in range(CHUNKS):
            for copy in z_coming[chunk]:
                copy.wait_recv()
            carry = jnp.zeros((16, cw), jnp.float32)
            for k in range(nz):
                longer = pz[k, :, columns(chunk)] * carry + trecv[k, :, columns(chunk)].astype(jnp.float32)
                carry = jnp.where(k < z, longer, carry)
            for k in range(ny):
                csend[k, :, columns(chunk)] = carry.astype(jnp.bfloat16)
                carry = gy[k, :, columns(chunk)] * carry + drecv[k, :, columns(chunk)].astype(jnp.float32)
            crecv[rows_of(y), columns(chunk)] = csend[y, :, columns(chunk)]
            y2_coming.append([
                send(
                    csend.at[(y + k) % ny, :, columns(chunk)], crecv.at[rows_of(y), columns(chunk)],
                    y2_ss.at[chunk, k], y2_rs.at[chunk, k], at_y(k),
                )
                for k in ydeltas
            ])
        for chunk in range(CHUNKS):
            for copy in y2_coming[chunk]:
                copy.wait_recv()
        c_out[...] = crecv[...]
        for copy in sends:
            copy.wait_send()
        for j in range(NX):

            @pl.when(x != j)
            def _(copy=home[j]):
                copy.wait_send()

    bf16, f32 = jnp.bfloat16, jnp.float32
    dma = pltpu.SemaphoreType.DMA
    scratch = [
        pltpu.VMEM((NX, 128, D), bf16),
        pltpu.VMEM((2, NX, 2, 128, 384), bf16),
        pltpu.VMEM((2, NX, 2, 64, D), bf16),
        pltpu.VMEM((2, NB, 128, 256), bf16),
        pltpu.VMEM((NX, 256, 128), bf16),
        pltpu.VMEM((NX, NX, 128, 128), bf16),
        pltpu.VMEM((NX, 128, 128), bf16),
        pltpu.VMEM((NX, 128, 128), bf16),
        pltpu.VMEM((NX, 128, D), f32),
        pltpu.VMEM((NX, 128, D), bf16),
        pltpu.VMEM((NX, 128, 640), f32),
        pltpu.VMEM((NB, 1, 128), jnp.int32),
        pltpu.VMEM((ny, 1, D), f32),
        pltpu.VMEM((nz, 1, D), f32),
        pltpu.VMEM((128, D), bf16),
        pltpu.VMEM((ny, 16, D), bf16),
        pltpu.VMEM((nz, 16, D), bf16),
        pltpu.VMEM((ny, 16, D), bf16),
        pltpu.VMEM((128, D), bf16),
        dma((9,)),
        dma((2, 4, 3)), dma((2, 4, 3)), dma((2,)), dma((2,)),
        dma((4, 2)), dma((4, 2)), dma((8,)), dma((8,)),
        dma((2, 4)), dma((2, 4)), dma((2,)), dma((2,)),
        dma((2, 4)), dma((2, 4)), dma((4, 4)), dma((4, 4)), dma((4,)), dma((4,)),
        dma((8,)), dma((8,)), dma((8,)), dma((8,)),
        dma((CHUNKS, 8)), dma((CHUNKS, 8)), dma((CHUNKS, 8)), dma((CHUNKS, 8)), dma((CHUNKS, 8)), dma((CHUNKS, 8)),
    ]
    anywhere, vmem = pl.BlockSpec(memory_space=pl.ANY), pl.BlockSpec(memory_space=pltpu.VMEM)
    return pl.pallas_call(
        kernel,
        out_shape=(jax.ShapeDtypeStruct((128, D), bf16), jax.ShapeDtypeStruct((128, D), f32)),
        in_specs=[anywhere] * 3 + [vmem] * 3,
        out_specs=(vmem, vmem),
        scratch_shapes=scratch,
        compiler_params=pltpu.CompilerParams(
            collective_id=0, has_side_effects=True, vmem_limit_bytes=40 << 20
        ),
        cost_estimate=pl.CostEstimate(
            flops=3_000_000_000, bytes_accessed=4_000_000, transcendentals=2_000_000
        ),
    )


def solution(mesh):
    layers = mesh.shape["layer"]
    ny = min(RING, layers)
    nz = layers // ny
    call = make_kernel(ny, nz)

    def per_device(states, w_qkv, w_out, gains, coarse_gain, doc_ids):
        entering, source = call(states, w_qkv, w_out, gains, coarse_gain, doc_ids.reshape(1, -1))
        first = lax.axis_index("layer") == 0
        entering = entering.astype(jnp.float32)
        state = states[0].astype(jnp.float32)
        corrected = entering + jnp.where(first, state, 0.0)
        ends = coarse_gain * entering + source
        return corrected[None], ends[None]

    in_specs = (
        P("layer", "tok", None),
        P("layer", "tok", None),
        P("layer", "tok", None),
        P("layer", None),
        P("layer", None),
        P("tok"),
    )
    out_specs = (P("layer", "tok", None), P("layer", "tok", None))
    return jax.shard_map(
        per_device, mesh=mesh, in_specs=in_specs, out_specs=out_specs, check_vma=False
    )
```

time: 606 us -> 85.4 us (0.14)
  waiting for transfers between devices: 403 us -> 0 us
  other arithmetic: 95.8 us -> 1.12 us
  Pallas kernels: 0 us -> 78.8 us
  blocking collectives: 50.9 us -> 0 us
  matrix products: 23.1 us -> 0 us
  between operations: 14 us -> 0.67 us
  local copies, waits for them, and re-layouts: 11.7 us -> 3.71 us
    all_gather x9 -> x0, waiting for transfers between devices: 401 us -> none  [the longest x1 182 us: entering(): pieces = jax.tree.map(lambda part: lax.all_gather(part, axis), value)]
    select_n x63 -> x0, other arithmetic: 93.4 us -> none  [lap(): jnp.where(position < mine, new, old)]
    pallas_call x0 -> x1, Pallas kernels: none -> 78.8 us  [per_device(): call(states, w_qkv, w_out, gains, coarse_gain, doc_ids.reshape(1, -1))]
    all_gather x2 -> x0, blocking collectives: 50.9 us -> none  [the longest x1 41.5 us: entering(): pieces = jax.tree.map(lambda part: lax.all_gather(part, axis), value)]
    dot_general x6 -> x0, matrix products: 15.4 us -> none  [the longest x2 6.26 us: attention(): jnp.einsum('hqk,khd->qhd', probs, values, preferred_element_type=jnp.floa...]
    sub x2 -> x0, matrix products: 7.75 us -> none  [attention(): expo = jnp.where(allowed[None], jnp.exp(scores - peak), 0.0)]
  transfers between devices with their start and end apart: 10 -> 0, of which waited for: 9 -> 0; matrix products, arithmetic and copies ran while one was open for 4% -> 0% of each run, Pallas kernels for 0% -> 0%
where the time goes in v1:
time: 85.4 us; the launch traced here: 84.3 us
  Pallas kernels  78.8 us (92%)
  local copies, waits for them, and re-layouts  3.71 us (4%)
  other arithmetic  1.12 us (1%)
    pallas_call x1, Pallas kernels, per_device(): call(states, w_qkv, w_out, gains, coarse_gain, doc_ids.reshape(1, -1))  78.8 us
    unnamed x12, local copies, waits for them, and re-layouts  3.71 us

profile of v1, /device:TPU:1, one launch (start us, length us, event | category | flops | bytes accessed | tf_op | source)
XLA Modules:
  0.0 84.3 jit_solution(3822001145508995313)
XLA Ops:
  0.6 0.0 copy-start.4
  0.6 0.0 copy-start.1
  0.7 0.0 copy-start.5
  0.7 0.7 copy-done.4
  1.3 0.0 copy-done.1
  1.3 0.0 copy-done.5
  1.3 0.0 copy-start
  1.3 0.9 %copy-done = bf16[1,128,1024]{2,1,0:T(8,128)(2,1)S(1)} copy-done((bf16[1,128,1024]{2,1,0:T(8,128)(2,1)S(1)}, bf16[1,128,1024]{2,1,0:T(8,128)(2,1)}, u32[]{:S(2)}) %copy-start) | copy-done | bytes 262168
  2.3 0.0 copy-start.2
  2.3 1.1 %copy-done.2 = bf16[2,128,1536]{2,1,0:T(8,128)(2,1)S(1)} copy-done((bf16[2,128,1536]{2,1,0:T(8,128)(2,1)S(1)}, bf16[2,128,1536]{2,1,0:T(8,128)(2,1)}, u32[]{:S(2)}) %copy-start.2) | copy-done | bytes 786456
  3.4 0.0 copy-start.3
  3.4 0.9 %copy-done.3 = bf16[2,64,1024]{2,1,0:T(8,128)(2,1)S(1)} copy-done((bf16[2,64,1024]{2,1,0:T(8,128)(2,1)S(1)}, bf16[2,64,1024]{2,1,0:T(8,128)(2,1)}, u32[]{:S(2)}) %copy-start.3) | copy-done | bytes 262168
  4.4 78.8 %shard_map.77 = (bf16[128,1024]{1,0:T(8,128)(2,1)S(1)}, f32[128,1024]{1,0:T(8,128)S(1)}) custom-call(bf16[1,128,1024]{2,1,0:T(8,128)(2,1)S(1)} %copy-done, bf16[2,128,1536]{2,1,0:T(8,128)(2,1)S(1)} %copy-done.2, bf16[2,64,1024]{2,1,0:T(8,128)(2,1)S(1)} %copy-done.3, f32[2,1024]{1,0:T(2,128)S(1)} %copy-done.4, f32[1,1024]{1,0:T(1,128)S(1)} %copy-done.1, ...), custom_call_target="tpu_custom_call" | custom-call | flops 3000000000 | bytes 4000000 | tf_op jit(solution)/shard_map/pallas_call | solution.py:404
  83.1 1.1 %fusion.2 = (f32[1,128,1024]{2,1,0:T(8,128)}, f32[1,128,1024]{2,1,0:T(8,128)}) fusion(f32[128,1024]{1,0:T(8,128)S(1)} %get-tuple-element.5, bf16[128,1024]{1,0:T(8,128)(2,1)S(1)} %get-tuple-element.4, f32[1024]{0:T(1024)S(1)} %bitcast.8, bf16[1,128,1024]{2,1,0:T(8,128)(2,1)S(1)} %copy-done, pred[]{:T(512)S(6)} %eq.3), kind=kLoop, calls=%fused_computation.4 | loop fusion | flops 786432 | bytes 2101249 | tf_op jit(solution)/shard_map/broadcast_in_dim | solution.py:410
Async XLA Ops:
  0.6 0.7 copy-start.4
  0.6 0.7 copy-start.1
  0.7 0.7 copy-start.5
  1.3 1.0 %copy-start = (bf16[1,128,1024]{2,1,0:T(8,128)(2,1)S(1)}, bf16[1,128,1024]{2,1,0:T(8,128)(2,1)}, u32[]{:S(2)}) copy-start(bf16[1,128,1024]{2,1,0:T(8,128)(2,1)} %states.1) | copy-start | bytes 786436
  2.3 1.1 %copy-start.2 = (bf16[2,128,1536]{2,1,0:T(8,128)(2,1)S(1)}, bf16[2,128,1536]{2,1,0:T(8,128)(2,1)}, u32[]{:S(2)}) copy-start(bf16[2,128,1536]{2,1,0:T(8,128)(2,1)} %w_qkv.1) | copy-start | bytes 2359300
  3.4 0.9 %copy-start.3 = (bf16[2,64,1024]{2,1,0:T(8,128)(2,1)S(1)}, bf16[2,64,1024]{2,1,0:T(8,128)(2,1)}, u32[]{:S(2)}) copy-start(bf16[2,64,1024]{2,1,0:T(8,128)(2,1)} %w_out.1) | copy-start | bytes 786436

commit v2 on v1

--- a/solution.py
+++ b/solution.py
@@ -12,7 +12,7 @@
 NX = 4
 NB = 8
 RING = 8
-CHUNKS = 2
+CHUNKS = 4
 EXP2_SCALE = math.log2(math.e) / 8.0
 FAR_FIRST = (4, 3, 5, 2, 6, 1, 7)
 
@@ -26,10 +26,10 @@
     cw = D // CHUNKS
 
     def kernel(
-        states, w_qkv, w_out, gains, coarse, doc_ids,
+        states, w_qkv, w_out, gains_in, coarse_in, doc_ids,
         c_out, d_out,
-        sx, wq, wo, kv, q2, o1, o2s, o2, x2, nx2, bias, docs,
-        gy, pz, dsend, drecv, trecv, csend, crecv,
+        sx, wq, wo, kv, q2, o1, o2s, o2, x2, bias, docs,
+        gains, gy, pz, dsend, drecv, trecv, csend, crecv,
         loc, w_ss, w_rs, wr_ss, wr_rs, s_ss, s_rs, doc_ss, doc_rs,
         wo_ss, wo_rs, wor_ss, wor_rs, kv_ss, kv_rs, o1_ss, o1_rs, o2_ss, o2_rs,
         g_ss, g_rs, p_ss, p_rs, y1_ss, y1_rs, z_ss, z_rs, y2_ss, y2_rs,
@@ -84,26 +84,32 @@
             copy = pltpu.make_async_copy(w_out.at[inner], wo.at[inner, x, c], loc.at[7 + inner])
             copy.start()
             own_wo.append(copy)
-        docs[tok] = doc_ids[...]
-        gy[y] = coarse[...]
+        own_small = [
+            pltpu.make_async_copy(doc_ids, docs.at[tok], loc.at[9]),
+            pltpu.make_async_copy(coarse_in, gy.at[y], loc.at[10]),
+            pltpu.make_async_copy(gains_in, gains, loc.at[11]),
+        ]
+        for copy in own_small:
+            copy.start()
 
         barrier = pltpu.get_barrier_semaphore()
         partners = [sibling] + [at_x(k) for k in (2, 1, 3)]
         partners += [at_y(k) for k in ydeltas] + [at_z(k) for k in zdeltas]
         for partner in partners:
             pl.semaphore_signal(barrier, inc=1, device_id=partner, device_id_type=MESH)
+        for copy in own_small:
+            copy.wait()
         pl.semaphore_wait(barrier, len(partners))
 
-        def send_wq(inner):
-            found = []
-            for delta in (2, 1, 3):
-                for part in range(3):
-                    found.append(send(
-                        w_qkv.at[inner, :, pl.ds(pl.multiple_of(part * 512 + 128 * chip(delta), 128), 128)],
-                        wq.at[inner, x, c, :, pl.ds(128 * part, 128)],
-                        w_ss.at[inner, delta, part], w_rs.at[inner, delta, part], at_x(delta),
-                    ))
-            return found
+        def send_wq_to(inner, delta):
+            return [
+                send(
+                    w_qkv.at[inner, :, pl.ds(pl.multiple_of(part * 512 + 128 * chip(delta), 128), 128)],
+                    wq.at[inner, x, c, :, pl.ds(128 * part, 128)],
+                    w_ss.at[inner, delta, part], w_rs.at[inner, delta, part], at_x(delta),
+                )
+                for part in range(3)
+            ]
 
         def share_wq(inner, arriving):
             for copy in own_wq[inner]:
@@ -113,10 +119,22 @@
             return send(wq.at[inner, :, c], wq.at[inner, :, c], wr_ss.at[inner], wr_rs.at[inner], sibling)
 
         def send_wo(inner):
-            return [
-                send(w_out.at[inner], wo.at[inner, x, c], wo_ss.at[inner, k], wo_rs.at[inner, k], at_x(k))
-                for k in (2, 1, 3)
-            ]
+            def part(delta, number):
+                rows = pl.ds(32 * number, 32)
+                return send(
+                    w_out.at[inner, rows], wo.at[inner, x, c, rows],
+                    wo_ss.at[inner, delta, number], wo_rs.at[inner, delta, number], at_x(delta),
+                )
+
+            return part(1, 0), part(3, 1), part(1, 1), part(3, 0)
+
+        def forward_wo(inner, arriving):
+            found = [arriving[2], arriving[3]]
+            for number, origin, target in ((0, 3, 1), (1, 1, 3)):
+                arriving[number].wait_recv()
+                block = wo.at[inner, chip(origin), c, pl.ds(32 * number, 32)]
+                found.append(send(block, block, wo_ss.at[inner, 2, number], wo_rs.at[inner, 2, number], at_x(target)))
+            return found
 
         def share_wo(inner, arriving):
             own_wo[inner].wait()
@@ -124,9 +142,9 @@
                 copy.wait_recv()
             return send(wo.at[inner, :, c], wo.at[inner, :, c], wor_ss.at[inner], wor_rs.at[inner], sibling)
 
-        wq_coming = send_wq(0)
+        wq_coming = send_wq_to(0, 2) + send_wq_to(0, 1) + send_wq_to(0, 3)
         doc_coming = [
-            send(doc_ids, docs.at[tok], doc_ss.at[k], doc_rs.at[k], at_x(k)) for k in (2, 1, 3)
+            send(docs.at[tok], docs.at[tok], doc_ss.at[k], doc_rs.at[k], at_x(k)) for k in (2, 1, 3)
         ]
 
         def half(delta, number):
@@ -137,7 +155,7 @@
 
         from_left_0, from_right_1 = half(1, 0), half(3, 1)
         from_left_1, from_right_0 = half(1, 1), half(3, 0)
-        gain_coming = [send(coarse, gy.at[y], g_ss.at[k], g_rs.at[k], at_y(k)) for k in ydeltas]
+        gain_coming = [send(gy.at[y], gy.at[y], g_ss.at[k], g_rs.at[k], at_y(k)) for k in ydeltas]
 
         for copy in doc_coming:
             copy.wait_recv()
@@ -211,6 +229,8 @@
         left_two.wait_recv()
         right_two.wait_recv()
         first_qkv(2)
+        wo_coming = forward_wo(0, wo_coming)
+        wq_coming = send_wq_to(1, 2) + send_wq_to(1, 1) + send_wq_to(1, 3)
 
         def attention(inner, j):
             count = 128 * key_blocks[j]
@@ -235,11 +255,21 @@
         for j in range(NX):
             o1[x, j] = attention(0, j)
             o1_coming.append([
-                send(o1.at[x, j], o1.at[x, j], o1_ss.at[j, k], o1_rs.at[j, k], at_x(k)) for k in (2, 1, 3)
+                send(o1.at[x, j], o1.at[x, j], o1_ss.at[j, k], o1_rs.at[j, k], at_x(k)) for k in (1, 3)
             ])
-        wq_coming = send_wq(1)
+
+        def forward_o1(j):
+            came, origin, target = (0, 3, 1) if j < 2 else (1, 1, 3)
+            o1_coming[j][came].wait_recv()
+            block = o1.at[chip(origin), j]
+            passed = send(block, block, o1_ss.at[j, 2], o1_rs.at[j, 2], at_x(target))
+            o1_coming[j] = [o1_coming[j][1 - came], passed]
+
         wo_shared = share_wo(0, wo_coming)
+        for j in range(NX):
+            forward_o1(j)
         wo_coming = send_wo(1)
+        wq_shared = share_wq(1, wq_coming)
         wo_shared.wait_recv()
 
         for j in range(NX):
@@ -250,11 +280,9 @@
                 heads, wo[0].reshape(512, D), preferred_element_type=jnp.float32
             )
             x2[j] = value
-            nx2[j] = rms(value, gains[1:2, :])
-
-        share_wq(1, wq_coming).wait_recv()
-        for j in range(NX):
-            qkv = jnp.dot(nx2[j], wq[1].reshape(D, 384), preferred_element_type=jnp.float32)
+            if j == 0:
+                wq_shared.wait_recv()
+            qkv = jnp.dot(rms(value, gains[1:2, :]), wq[1].reshape(D, 384), preferred_element_type=jnp.float32)
             keep_qkv(1, j, qkv)
             block = 2 * j + c
             kv_shared[1].append(
@@ -262,6 +290,7 @@
             )
         for copy in kv_shared[1]:
             copy.wait_recv()
+        wo_coming = forward_wo(1, wo_coming)
         home = []
         for j in range(NX):
             o2s[j] = attention(1, j)
@@ -279,7 +308,7 @@
         heads = jnp.concatenate([o2[k] for k in range(NX)], axis=1)
         value = x2[x] + jnp.dot(heads, wo[1].reshape(512, D), preferred_element_type=jnp.float32)
         start = jnp.where(layer == 0, 0.0, sx[x].astype(jnp.float32))
-        value = value - coarse[...] * start
+        value = value - gy[y] * start
         d_out[...] = value
         dsend[...] = value.astype(jnp.bfloat16)
 
@@ -360,9 +389,9 @@
         pltpu.VMEM((NX, 128, 128), bf16),
         pltpu.VMEM((NX, 128, 128), bf16),
         pltpu.VMEM((NX, 128, D), f32),
-        pltpu.VMEM((NX, 128, D), bf16),
         pltpu.VMEM((NX, 128, 640), f32),
         pltpu.VMEM((NB, 1, 128), jnp.int32),
+        pltpu.VMEM((2, D), f32),
         pltpu.VMEM((ny, 1, D), f32),
         pltpu.VMEM((nz, 1, D), f32),
         pltpu.VMEM((128, D), bf16),
@@ -370,23 +399,23 @@
         pltpu.VMEM((nz, 16, D), bf16),
         pltpu.VMEM((ny, 16, D), bf16),
         pltpu.VMEM((128, D), bf16),
-        dma((9,)),
+        dma((12,)),
         dma((2, 4, 3)), dma((2, 4, 3)), dma((2,)), dma((2,)),
         dma((4, 2)), dma((4, 2)), dma((8,)), dma((8,)),
-        dma((2, 4)), dma((2, 4)), dma((2,)), dma((2,)),
+        dma((2, 4, 2)), dma((2, 4, 2)), dma((2,)), dma((2,)),
         dma((2, 4)), dma((2, 4)), dma((4, 4)), dma((4, 4)), dma((4,)), dma((4,)),
         dma((8,)), dma((8,)), dma((8,)), dma((8,)),
         dma((CHUNKS, 8)), dma((CHUNKS, 8)), dma((CHUNKS, 8)), dma((CHUNKS, 8)), dma((CHUNKS, 8)), dma((CHUNKS, 8)),
     ]
-    anywhere, vmem = pl.BlockSpec(memory_space=pl.ANY), pl.BlockSpec(memory_space=pltpu.VMEM)
+    anywhere, vmem = pl.BlockSpec(memory_space=pltpu.HBM), pl.BlockSpec(memory_space=pltpu.VMEM)
     return pl.pallas_call(
         kernel,
         out_shape=(jax.ShapeDtypeStruct((128, D), bf16), jax.ShapeDtypeStruct((128, D), f32)),
-        in_specs=[anywhere] * 3 + [vmem] * 3,
+        in_specs=[anywhere] * 6,
         out_specs=(vmem, vmem),
         scratch_shapes=scratch,
         compiler_params=pltpu.CompilerParams(
-            collective_id=0, has_side_effects=True, vmem_limit_bytes=40 << 20
+            collective_id=0, has_side_effects=True, vmem_limit_bytes=60 << 20
         ),
         cost_estimate=pl.CostEstimate(
             flops=3_000_000_000, bytes_accessed=4_000_000, transcendentals=2_000_000

time: 85.4 us -> 79.6 us (0.932); the launches traced: 84.3 us -> 79.4 us
  local copies, waits for them, and re-layouts: 3.71 us -> 0.01 us
  Pallas kernels: 78.8 us -> 76.5 us
  other arithmetic: 1.12 us -> 2.23 us
    unnamed x12 -> x4, local copies, waits for them, and re-layouts: 3.71 us -> 0.01 us
    pallas_call x1, Pallas kernels: 78.8 us -> 76.5 us  [per_device(): call(states, w_qkv, w_out, gains, coarse_gain, doc_ids.reshape(1, -1))]
    broadcast_in_dim x1, other arithmetic: 1.12 us -> 2.23 us  [per_device(): return (corrected[None], ends[None])]
where the time goes in v2:
time: 79.6 us; the launch traced here: 79.4 us
  Pallas kernels  76.5 us (96%)
  other arithmetic  2.23 us (3%)
    pallas_call x1, Pallas kernels, per_device(): call(states, w_qkv, w_out, gains, coarse_gain, doc_ids.reshape(1, -1))  76.5 us
    broadcast_in_dim x1, other arithmetic, per_device(): return (corrected[None], ends[None])  2.23 us

profile of v2, /device:TPU:1, one launch (start us, length us, event | category | flops | bytes accessed | tf_op | source)
XLA Modules:
  0.0 79.4 jit_solution(6010307909347458293)
XLA Ops:
  0.6 0.0 copy-start
  0.6 0.0 copy-start.1
  0.7 76.5 %shard_map.77 = (bf16[128,1024]{1,0:T(8,128)(2,1)}, f32[128,1024]{1,0:T(8,128)}) custom-call(bf16[1,128,1024]{2,1,0:T(8,128)(2,1)} %states.1, bf16[2,128,1536]{2,1,0:T(8,128)(2,1)} %w_qkv.1, bf16[2,64,1024]{2,1,0:T(8,128)(2,1)} %w_out.1, f32[2,1024]{1,0:T(2,128)} %gains_in.1, f32[1,1024]{1,0:T(1,128)} %coarse_in.1, s32[1,128]{1,0:T(1,128)} %bitcast.9), custom_call_target="tpu_custom_call" | custom-call | flops 3000000000 | bytes 4000000 | tf_op jit(solution)/shard_map/pallas_call | solution.py:433
  77.2 0.0 copy-done
  77.2 0.0 copy-done.1
  77.2 2.2 %fusion.2 = (f32[1,128,1024]{2,1,0:T(8,128)}, f32[1,128,1024]{2,1,0:T(8,128)}) fusion(f32[128,1024]{1,0:T(8,128)} %get-tuple-element.5, bf16[128,1024]{1,0:T(8,128)(2,1)} %get-tuple-element.4, f32[1024]{0:T(1024)S(1)} %bitcast.8, bf16[1,128,1024]{2,1,0:T(8,128)(2,1)S(1)} %copy-done, pred[]{:T(512)S(6)} %eq.3), kind=kLoop, calls=%fused_computation.4 | loop fusion | flops 786432 | bytes 2101249 | tf_op jit(solution)/shard_map/broadcast_in_dim | solution.py:439
Async XLA Ops:
  0.6 76.5 %copy-start = (bf16[1,128,1024]{2,1,0:T(8,128)(2,1)S(1)}, bf16[1,128,1024]{2,1,0:T(8,128)(2,1)}, u32[]{:S(2)}) copy-start(bf16[1,128,1024]{2,1,0:T(8,128)(2,1)} %states.1) | copy-start | bytes 786436
  0.6 76.5 %copy-start.1 = (f32[1,1024]{1,0:T(1,128)S(1)}, f32[1,1024]{1,0:T(1,128)}, u32[]{:S(2)}) copy-start(f32[1,1024]{1,0:T(1,128)} %coarse_in.1) | copy-start | bytes 12292

commit v3 on v2

--- a/solution.py
+++ b/solution.py
@@ -255,20 +255,12 @@
         for j in range(NX):
             o1[x, j] = attention(0, j)
             o1_coming.append([
-                send(o1.at[x, j], o1.at[x, j], o1_ss.at[j, k], o1_rs.at[j, k], at_x(k)) for k in (1, 3)
+                send(o1.at[x, j], o1.at[x, j], o1_ss.at[j, k], o1_rs.at[j, k], at_x(k)) for k in (2, 1, 3)
             ])
 
-        def forward_o1(j):
-            came, origin, target = (0, 3, 1) if j < 2 else (1, 1, 3)
-            o1_coming[j][came].wait_recv()
-            block = o1.at[chip(origin), j]
-            passed = send(block, block, o1_ss.at[j, 2], o1_rs.at[j, 2], at_x(target))
-            o1_coming[j] = [o1_coming[j][1 - came], passed]
-
+        wo_next = send_wo(1)
         wo_shared = share_wo(0, wo_coming)
-        for j in range(NX):
-            forward_o1(j)
-        wo_coming = send_wo(1)
+        wo_coming = wo_next
         wq_shared = share_wq(1, wq_coming)
         wo_shared.wait_recv()
 
@@ -280,6 +272,8 @@
                 heads, wo[0].reshape(512, D), preferred_element_type=jnp.float32
             )
             x2[j] = value
+            if j == 3:
+                wo_coming = forward_wo(1, wo_coming)
             if j == 0:
                 wq_shared.wait_recv()
             qkv = jnp.dot(rms(value, gains[1:2, :]), wq[1].reshape(D, 384), preferred_element_type=jnp.float32)
@@ -290,9 +284,10 @@
             )
         for copy in kv_shared[1]:
             copy.wait_recv()
-        wo_coming = forward_wo(1, wo_coming)
         home = []
         for j in range(NX):
+            if j == 3:
+                wo_shared = share_wo(1, wo_coming)
             o2s[j] = attention(1, j)
             copy = remote(o2s.at[j], o2.at[x], o2_ss.at[j], o2_rs.at[x], (layer, 2 * j + c))
             home.append(copy)
@@ -302,7 +297,7 @@
                 copy.start()
 
         o2[x] = o2s[x]
-        share_wo(1, wo_coming).wait_recv()
+        wo_shared.wait_recv()
         for delta in (1, 2, 3):
             pltpu.make_async_copy(o2s.at[0], o2.at[chip(delta)], o2_rs.at[chip(delta)]).wait()
         heads = jnp.concatenate([o2[k] for k in range(NX)], axis=1)
@@ -415,7 +410,7 @@
         out_specs=(vmem, vmem),
         scratch_shapes=scratch,
         compiler_params=pltpu.CompilerParams(
-            collective_id=0, has_side_effects=True, vmem_limit_bytes=60 << 20
+            collective_id=0, has_side_effects=True, vmem_limit_bytes=40 << 20
         ),
         cost_estimate=pl.CostEstimate(
             flops=3_000_000_000, bytes_accessed=4_000_000, transcendentals=2_000_000
@@ -430,7 +425,8 @@
     call = make_kernel(ny, nz)
 
     def per_device(states, w_qkv, w_out, gains, coarse_gain, doc_ids):
-        entering, source = call(states, w_qkv, w_out, gains, coarse_gain, doc_ids.reshape(1, -1))
+        hold = [pltpu.with_memory_space_constraint(v, pltpu.HBM) for v in (states, w_qkv, w_out, gains, coarse_gain, doc_ids.reshape(1, -1))]
+        entering, source = call(*hold)
         first = lax.axis_index("layer") == 0
         entering = entering.astype(jnp.float32)
         state = states[0].astype(jnp.float32)

time: 79.6 us -> 76.2 us (0.957)
  Pallas kernels: 76.5 us -> 73.5 us
  other arithmetic: 2.23 us -> 1.13 us
    pallas_call x1, Pallas kernels: 76.5 us -> 73.5 us  [per_device(): entering, source = call(*hold)]
    broadcast_in_dim x1, other arithmetic: 2.23 us -> 1.13 us  [per_device(): return (corrected[None], ends[None])]
where the time goes in v3:
time: 76.2 us; the launch traced here: 75.4 us
  Pallas kernels  73.5 us (96%)
  other arithmetic  1.13 us (1%)
    pallas_call x1, Pallas kernels, per_device(): entering, source = call(*hold)  73.5 us

profile of v3, /device:TPU:1, one launch (start us, length us, event | category | flops | bytes accessed | tf_op | source)
XLA Modules:
  0.0 75.4 jit_solution(13668180885996328165)
XLA Ops:
  0.6 0.0 copy-start
  0.6 0.0 copy-start.1
  0.7 73.5 %shard_map.77 = (bf16[128,1024]{1,0:T(8,128)(2,1)S(1)}, f32[128,1024]{1,0:T(8,128)S(1)}) custom-call(bf16[1,128,1024]{2,1,0:T(8,128)(2,1)} %states.1, bf16[2,128,1536]{2,1,0:T(8,128)(2,1)} %w_qkv.1, bf16[2,64,1024]{2,1,0:T(8,128)(2,1)} %w_out.1, f32[2,1024]{1,0:T(2,128)} %gains_in.1, f32[1,1024]{1,0:T(1,128)} %coarse_in.1, s32[1,128]{1,0:T(1,128)} %bitcast.9), custom_call_target="tpu_custom_call" | custom-call | flops 3000000000 | bytes 4000000 | tf_op jit(solution)/shard_map/pallas_call | solution.py:429
  74.2 0.0 copy-done
  74.2 0.0 copy-done.1
  74.2 1.1 %fusion.2 = (f32[1,128,1024]{2,1,0:T(8,128)}, f32[1,128,1024]{2,1,0:T(8,128)}) fusion(f32[128,1024]{1,0:T(8,128)S(1)} %get-tuple-element.5, bf16[128,1024]{1,0:T(8,128)(2,1)S(1)} %get-tuple-element.4, f32[1024]{0:T(1024)S(1)} %bitcast.8, bf16[1,128,1024]{2,1,0:T(8,128)(2,1)S(1)} %copy-done, pred[]{:T(512)S(6)} %eq.3), kind=kLoop, calls=%fused_computation.4 | loop fusion | flops 786432 | bytes 2101249 | tf_op jit(solution)/shard_map/broadcast_in_dim | solution.py:435
Async XLA Ops:
  0.6 73.6 %copy-start = (bf16[1,128,1024]{2,1,0:T(8,128)(2,1)S(1)}, bf16[1,128,1024]{2,1,0:T(8,128)(2,1)}, u32[]{:S(2)}) copy-start(bf16[1,128,1024]{2,1,0:T(8,128)(2,1)} %states.1) | copy-start | bytes 786436
  0.6 73.6 %copy-start.1 = (f32[1,1024]{1,0:T(1,128)S(1)}, f32[1,1024]{1,0:T(1,128)}, u32[]{:S(2)}) copy-start(f32[1,1024]{1,0:T(1,128)} %coarse_in.1) | copy-start | bytes 12292

commit v4 on v3

--- a/solution.py
+++ b/solution.py
@@ -35,21 +35,25 @@
         g_ss, g_rs, p_ss, p_rs, y1_ss, y1_rs, z_ss, z_rs, y2_ss, y2_rs,
     ):
         layer, tok = lax.axis_index("layer"), lax.axis_index("tok")
-        x, c = tok // 2, tok % 2
-        z, y = layer // ny, layer % ny
+        x, c = lax.div(tok, 2), lax.rem(tok, 2)
+        z, y = lax.div(layer, ny), lax.rem(layer, ny)
         sibling = (layer, 2 * x + 1 - c)
 
+        chips = [lax.rem(x + k, NX) for k in range(NX)]
+        ring_y = [lax.rem(y + k, ny) for k in range(ny)]
+        ring_z = [lax.rem(z + k, nz) for k in range(nz)]
+
         def chip(delta):
-            return (x + delta) % NX
+            return chips[delta]
 
         def at_x(delta):
-            return (layer, 2 * chip(delta) + c)
+            return (layer, 2 * chips[delta] + c)
 
         def at_y(delta):
-            return (z * ny + (y + delta) % ny, tok)
+            return (z * ny + ring_y[delta], tok)
 
         def at_z(delta):
-            return (((z + delta) % nz) * ny + y, tok)
+            return (ring_z[delta] * ny + y, tok)
 
         ydeltas = [k for k in FAR_FIRST if k < ny]
         zdeltas = [k for k in FAR_FIRST if k < nz]
@@ -310,41 +314,43 @@
         def columns(chunk):
             return pl.ds(cw * chunk, cw)
 
+        def start(*args):
+            remote(*args).start()
+
+        def arrived(ref, sem):
+            pltpu.make_async_copy(ref, ref, sem).wait()
+
+        def all_of(buffer, count, chunk, sem):
+            if count > 1:
+                arrived(buffer.at[pl.ds(0, count - 1), :, columns(chunk)], sem.at[chunk])
+
         def rows_of(position):
             return pl.ds(pl.multiple_of(16 * position, 16), 16)
 
-        y1_coming = [
-            [
-                send(
-                    dsend.at[rows_of((y + k) % ny), columns(chunk)], drecv.at[y, :, columns(chunk)],
-                    y1_ss.at[chunk, k], y1_rs.at[chunk, k], at_y(k),
+        for chunk in range(CHUNKS):
+            for k in ydeltas:
+                start(
+                    dsend.at[rows_of(ring_y[k]), columns(chunk)], drecv.at[y, :, columns(chunk)],
+                    y1_ss.at[chunk], y1_rs.at[chunk], at_y(k),
                 )
-                for k in ydeltas
-            ]
-            for chunk in range(CHUNKS)
-        ]
         drecv[y] = dsend[rows_of(y), :]
         for copy in product_coming:
             copy.wait_recv()
-        z_coming = []
-        for chunk in range(CHUNKS):
-            for copy in y1_coming[chunk]:
-                copy.wait_recv()
+        for copy in sends:
+            copy.wait_send()
+        for chunk in range(CHUNKS):
+            all_of(drecv, ny, chunk, y1_rs)
             total = jnp.zeros((16, cw), jnp.float32)
             for k in range(ny):
                 total = gy[k, :, columns(chunk)] * total + drecv[k, :, columns(chunk)].astype(jnp.float32)
             trecv[z, :, columns(chunk)] = total.astype(jnp.bfloat16)
-            z_coming.append([
-                send(
-                    trecv.at[z, :, columns(chunk)], trecv.at[z, :, columns(chunk)],
-                    z_ss.at[chunk, k], z_rs.at[chunk, k], at_z(k),
-                )
-                for k in zdeltas
-            ])
-        y2_coming = []
-        for chunk in range(CHUNKS):
-            for copy in z_coming[chunk]:
-                copy.wait_recv()
+            for k in zdeltas:
+                piece = trecv.at[z, :, columns(chunk)]
+                start(piece, piece, z_ss.at[chunk], z_rs.at[chunk], at_z(k))
+        for chunk in range(CHUNKS):
+            all_of(drecv, ny, chunk, y1_ss)
+        for chunk in range(CHUNKS):
+            all_of(trecv, nz, chunk, z_rs)
             carry = jnp.zeros((16, cw), jnp.float32)
             for k in range(nz):
                 longer = pz[k, :, columns(chunk)] * carry + trecv[k, :, columns(chunk)].astype(jnp.float32)
@@ -353,24 +359,24 @@
                 csend[k, :, columns(chunk)] = carry.astype(jnp.bfloat16)
                 carry = gy[k, :, columns(chunk)] * carry + drecv[k, :, columns(chunk)].astype(jnp.float32)
             crecv[rows_of(y), columns(chunk)] = csend[y, :, columns(chunk)]
-            y2_coming.append([
-                send(
-                    csend.at[(y + k) % ny, :, columns(chunk)], crecv.at[rows_of(y), columns(chunk)],
-                    y2_ss.at[chunk, k], y2_rs.at[chunk, k], at_y(k),
+            for k in ydeltas:
+                start(
+                    csend.at[ring_y[k], :, columns(chunk)], crecv.at[rows_of(y), columns(chunk)],
+                    y2_ss.at[chunk], y2_rs.at[chunk], at_y(k),
                 )
-                for k in ydeltas
-            ])
-        for chunk in range(CHUNKS):
-            for copy in y2_coming[chunk]:
-                copy.wait_recv()
-        c_out[...] = crecv[...]
-        for copy in sends:
-            copy.wait_send()
+        for chunk in range(CHUNKS):
+            all_of(trecv, nz, chunk, z_ss)
         for j in range(NX):
 
             @pl.when(x != j)
             def _(copy=home[j]):
                 copy.wait_send()
+
+        for chunk in range(CHUNKS):
+            all_of(csend, ny, chunk, y2_rs)
+        c_out[...] = crecv[...]
+        for chunk in range(CHUNKS):
+            all_of(csend, ny, chunk, y2_ss)
 
     bf16, f32 = jnp.bfloat16, jnp.float32
     dma = pltpu.SemaphoreType.DMA
@@ -400,7 +406,7 @@
         dma((2, 4, 2)), dma((2, 4, 2)), dma((2,)), dma((2,)),
         dma((2, 4)), dma((2, 4)), dma((4, 4)), dma((4, 4)), dma((4,)), dma((4,)),
         dma((8,)), dma((8,)), dma((8,)), dma((8,)),
-        dma((CHUNKS, 8)), dma((CHUNKS, 8)), dma((CHUNKS, 8)), dma((CHUNKS, 8)), dma((CHUNKS, 8)), dma((CHUNKS, 8)),
+        dma((CHUNKS,)), dma((CHUNKS,)), dma((CHUNKS,)), dma((CHUNKS,)), dma((CHUNKS,)), dma((CHUNKS,)),
     ]
     anywhere, vmem = pl.BlockSpec(memory_space=pltpu.HBM), pl.BlockSpec(memory_space=pltpu.VMEM)
     return pl.pallas_call(

time: 76.2 us -> 74.3 us (0.975)
  Pallas kernels: 73.5 us -> 71.7 us
    pallas_call x1, Pallas kernels: 73.5 us -> 71.7 us  [per_device(): entering, source = call(*hold)]
where the time goes in v4:
time: 74.3 us; the launch traced here: 73.5 us
  Pallas kernels  71.7 us (97%)
  other arithmetic  1.13 us (2%)
    pallas_call x1, Pallas kernels, per_device(): entering, source = call(*hold)  71.7 us

profile of v4, /device:TPU:1, one launch (start us, length us, event | category | flops | bytes accessed | tf_op | source)
XLA Modules:
  0.0 73.5 jit_solution(14238997482789802782)
XLA Ops:
  0.6 0.0 copy-start
  0.6 0.0 copy-start.1
  0.7 71.7 %shard_map.77 = (bf16[128,1024]{1,0:T(8,128)(2,1)S(1)}, f32[128,1024]{1,0:T(8,128)S(1)}) custom-call(bf16[1,128,1024]{2,1,0:T(8,128)(2,1)} %states.1, bf16[2,128,1536]{2,1,0:T(8,128)(2,1)} %w_qkv.1, bf16[2,64,1024]{2,1,0:T(8,128)(2,1)} %w_out.1, f32[2,1024]{1,0:T(2,128)} %gains_in.1, f32[1,1024]{1,0:T(1,128)} %coarse_in.1, s32[1,128]{1,0:T(1,128)} %bitcast.9), custom_call_target="tpu_custom_call" | custom-call | flops 3000000000 | bytes 4000000 | tf_op jit(solution)/shard_map/pallas_call | solution.py:435
  72.3 0.0 copy-done
  72.3 0.0 copy-done.1
  72.3 1.1 %fusion.2 = (f32[1,128,1024]{2,1,0:T(8,128)}, f32[1,128,1024]{2,1,0:T(8,128)}) fusion(f32[128,1024]{1,0:T(8,128)S(1)} %get-tuple-element.5, bf16[128,1024]{1,0:T(8,128)(2,1)S(1)} %get-tuple-element.4, f32[1024]{0:T(1024)S(1)} %bitcast.8, bf16[1,128,1024]{2,1,0:T(8,128)(2,1)S(1)} %copy-done, pred[]{:T(512)S(6)} %eq.3), kind=kLoop, calls=%fused_computation.4 | loop fusion | flops 786432 | bytes 2101249 | tf_op jit(solution)/shard_map/broadcast_in_dim | solution.py:441
Async XLA Ops:
  0.6 71.7 %copy-start = (bf16[1,128,1024]{2,1,0:T(8,128)(2,1)S(1)}, bf16[1,128,1024]{2,1,0:T(8,128)(2,1)}, u32[]{:S(2)}) copy-start(bf16[1,128,1024]{2,1,0:T(8,128)(2,1)} %states.1) | copy-start | bytes 786436
  0.6 71.7 %copy-start.1 = (f32[1,1024]{1,0:T(1,128)S(1)}, f32[1,1024]{1,0:T(1,128)}, u32[]{:S(2)}) copy-start(f32[1,1024]{1,0:T(1,128)} %coarse_in.1) | copy-start | bytes 12292

commit v5 on v4

--- a/solution.py
+++ b/solution.py
@@ -140,11 +140,20 @@
                 found.append(send(block, block, wo_ss.at[inner, 2, number], wo_rs.at[inner, 2, number], at_x(target)))
             return found
 
-        def share_wo(inner, arriving):
+        def share_near(inner, arriving):
             own_wo[inner].wait()
-            for copy in arriving:
+            for copy in arriving[:2]:
                 copy.wait_recv()
-            return send(wo.at[inner, :, c], wo.at[inner, :, c], wor_ss.at[inner], wor_rs.at[inner], sibling)
+            return [share_block(inner, k) for k in (0, 1, 3)]
+
+        def share_far(inner, arriving):
+            for copy in arriving[2:]:
+                copy.wait_recv()
+            return [share_block(inner, 2)]
+
+        def share_block(inner, delta):
+            block = wo.at[inner, chip(delta), c]
+            return send(block, block, wor_ss.at[inner, delta], wor_rs.at[inner, delta], sibling)
 
         wq_coming = send_wq_to(0, 2) + send_wq_to(0, 1) + send_wq_to(0, 3)
         doc_coming = [
@@ -263,10 +272,11 @@
             ])
 
         wo_next = send_wo(1)
-        wo_shared = share_wo(0, wo_coming)
+        wo_shared = share_near(0, wo_coming) + share_far(0, wo_coming)
         wo_coming = wo_next
         wq_shared = share_wq(1, wq_coming)
-        wo_shared.wait_recv()
+        for copy in wo_shared:
+            copy.wait_recv()
 
         for j in range(NX):
             for copy in o1_coming[j]:
@@ -290,8 +300,10 @@
             copy.wait_recv()
         home = []
         for j in range(NX):
+            if j == 2:
+                wo_shared = share_near(1, wo_coming)
             if j == 3:
-                wo_shared = share_wo(1, wo_coming)
+                wo_shared += share_far(1, wo_coming)
             o2s[j] = attention(1, j)
             copy = remote(o2s.at[j], o2.at[x], o2_ss.at[j], o2_rs.at[x], (layer, 2 * j + c))
             home.append(copy)
@@ -301,15 +313,11 @@
                 copy.start()
 
         o2[x] = o2s[x]
-        wo_shared.wait_recv()
+        for copy in wo_shared:
+            copy.wait_recv()
         for delta in (1, 2, 3):
             pltpu.make_async_copy(o2s.at[0], o2.at[chip(delta)], o2_rs.at[chip(delta)]).wait()
         heads = jnp.concatenate([o2[k] for k in range(NX)], axis=1)
-        value = x2[x] + jnp.dot(heads, wo[1].reshape(512, D), preferred_element_type=jnp.float32)
-        start = jnp.where(layer == 0, 0.0, sx[x].astype(jnp.float32))
-        value = value - gy[y] * start
-        d_out[...] = value
-        dsend[...] = value.astype(jnp.bfloat16)
 
         def columns(chunk):
             return pl.ds(cw * chunk, cw)
@@ -328,6 +336,14 @@
             return pl.ds(pl.multiple_of(16 * position, 16), 16)
 
         for chunk in range(CHUNKS):
+            part = columns(chunk)
+            value = x2[x, :, part] + jnp.dot(
+                heads, wo[1, :, :, :, part].reshape(512, cw), preferred_element_type=jnp.float32
+            )
+            entering = jnp.where(layer == 0, 0.0, sx[x, :, part].astype(jnp.float32))
+            value = value - gy[y, :, part] * entering
+            d_out[:, part] = value
+            dsend[:, part] = value.astype(jnp.bfloat16)
             for k in ydeltas:
                 start(
                     dsend.at[rows_of(ring_y[k]), columns(chunk)], drecv.at[y, :, columns(chunk)],
@@ -403,7 +419,7 @@
         dma((12,)),
         dma((2, 4, 3)), dma((2, 4, 3)), dma((2,)), dma((2,)),
         dma((4, 2)), dma((4, 2)), dma((8,)), dma((8,)),
-        dma((2, 4, 2)), dma((2, 4, 2)), dma((2,)), dma((2,)),
+        dma((2, 4, 2)), dma((2, 4, 2)), dma((2, 4)), dma((2, 4)),
         dma((2, 4)), dma((2, 4)), dma((4, 4)), dma((4, 4)), dma((4,)), dma((4,)),
         dma((8,)), dma((8,)), dma((8,)), dma((8,)),
         dma((CHUNKS,)), dma((CHUNKS,)), dma((CHUNKS,)), dma((CHUNKS,)), dma((CHUNKS,)), dma((CHUNKS,)),

time: 74.3 us -> 74.3 us (level)
  no operation moved by 1% of the time
where the time goes in v5:
time: 74.3 us; the launch traced here: 73 us
  Pallas kernels  71.2 us (96%)
  other arithmetic  1.13 us (2%)
    pallas_call x1, Pallas kernels, per_device(): entering, source = call(*hold)  71.2 us

profile of v5, /device:TPU:1, one launch (start us, length us, event | category | flops | bytes accessed | tf_op | source)
XLA Modules:
  0.0 73.0 jit_solution(15192350251237703922)
XLA Ops:
  0.6 0.0 copy-start
  0.6 0.0 copy-start.1
  0.7 71.2 %shard_map.77 = (bf16[128,1024]{1,0:T(8,128)(2,1)S(1)}, f32[128,1024]{1,0:T(8,128)S(1)}) custom-call(bf16[1,128,1024]{2,1,0:T(8,128)(2,1)} %states.1, bf16[2,128,1536]{2,1,0:T(8,128)(2,1)} %w_qkv.1, bf16[2,64,1024]{2,1,0:T(8,128)(2,1)} %w_out.1, f32[2,1024]{1,0:T(2,128)} %gains_in.1, f32[1,1024]{1,0:T(1,128)} %coarse_in.1, s32[1,128]{1,0:T(1,128)} %bitcast.9), custom_call_target="tpu_custom_call" | custom-call | flops 3000000000 | bytes 4000000 | tf_op jit(solution)/shard_map/pallas_call | solution.py:451
  71.9 0.0 copy-done
  71.9 0.0 copy-done.1
  71.9 1.1 %fusion.2 = (f32[1,128,1024]{2,1,0:T(8,128)}, f32[1,128,1024]{2,1,0:T(8,128)}) fusion(f32[128,1024]{1,0:T(8,128)S(1)} %get-tuple-element.5, bf16[128,1024]{1,0:T(8,128)(2,1)S(1)} %get-tuple-element.4, f32[1024]{0:T(1024)S(1)} %bitcast.8, bf16[1,128,1024]{2,1,0:T(8,128)(2,1)S(1)} %copy-done, pred[]{:T(512)S(6)} %eq.3), kind=kLoop, calls=%fused_computation.4 | loop fusion | flops 786432 | bytes 2101249 | tf_op jit(solution)/shard_map/broadcast_in_dim | solution.py:457
Async XLA Ops:
  0.6 71.3 %copy-start = (bf16[1,128,1024]{2,1,0:T(8,128)(2,1)S(1)}, bf16[1,128,1024]{2,1,0:T(8,128)(2,1)}, u32[]{:S(2)}) copy-start(bf16[1,128,1024]{2,1,0:T(8,128)(2,1)} %states.1) | copy-start | bytes 786436
  0.6 71.3 %copy-start.1 = (f32[1,1024]{1,0:T(1,128)S(1)}, f32[1,1024]{1,0:T(1,128)}, u32[]{:S(2)}) copy-start(f32[1,1024]{1,0:T(1,128)} %coarse_in.1) | copy-start | bytes 12292
